TPU v7x, 512 devices: a whole 4x8x8 slice. The times are simulated.
512 devices in a mesh: band: 64 (over x, z_hi, y), plane: 8 (over z_lo, core).
Axes of the slice: x: 4, y: 8, z: 8 (z_hi: 2, z_lo: 4; z = z_hi * 4 + z_lo), core: 2. Of those that a mesh axis runs over, the one named last changes fastest.
Arguments:
- orbitals: float32 [64, 128, 128, 128], P('band', 'plane'), may hold values from -6 to 6
- coulomb: bfloat16 [128, 21504], P(None, 'plane'), may hold values from 0.049804688 to 2
- stick_lists: int32 [8, 2688], replicated, may hold values from -1 to 16383, as said below
- roots: int32 [2], replicated, may hold values from 0 to 63
Outputs:
- exchange_field: bfloat16 [64, 128, 128, 128], P('band', 'plane')
Inputs may be any that keep to these rules, and one draw needn't show every extreme that they name: `stick_lists`: row o lists, slot by slot, the stick columns h * 128 + g that plane owner o holds, then -1 in its unused slots. The 12288 listed columns are distinct and are those with the smallest sum of squared signed frequencies. Every owner holds at least one stick; one owner holds exactly 2688.
All inputs are finite; a program needn't handle non-finite values.
Results may differ from a plain program's by a relative error of at most 0.0096.
Values may be sent and summed in bfloat16 or wider, within the bound.
A program may use at most 64 MiB of HBM per device.

v0:
```python
import functools
import math

import jax
import jax.numpy as jnp
import numpy as np
from jax import lax
from jax.experimental import pallas as pl
from jax.experimental.pallas import tpu as pltpu
from jax.sharding import PartitionSpec as P

NX, NZ, NY = 4, 2, 8
STICKS = 12288
GROUPS = 2
STEPS = 2
PIECES = 3
MESH = pl.DeviceIdType.MESH
F32, BF16 = jnp.float32, jnp.bfloat16


def cas_table(n):
    k = np.arange(n)
    angles = 2.0 * math.pi / n * ((k[:, None] * k[None, :]) % n)
    return np.asarray(np.cos(angles) + np.sin(angles), np.float32)


def pair_table(n, width):
    cas = cas_table(n)
    half = width // GROUPS
    table = np.zeros((2, n, GROUPS, n // width, 2, half), np.float32)
    by_x = cas.reshape(n, n // width, GROUPS, half).transpose(0, 2, 1, 3)
    for h in range(2):
        table[h, :, :, :, h, :] = by_x
    return table.reshape(2 * n, 2 * n)


def packing(n, n_plane):
    signed = np.minimum(np.arange(n), n - np.arange(n))
    squares = signed[:, None] ** 2 + signed[None, :] ** 2
    kept = (squares <= np.sort(squares.reshape(-1))[STICKS - 1]).sum(1)
    best = None
    for t in range(1, n // 2 + 1):
        for extra in ([], [n - t + 1]):
            second = [h for h in range(n) if kept[h] and (signed[h] >= t or h in extra)]
            firsts = [h for h in range(n) if kept[h] and h not in second]
            free, mate = sorted(firsts, key=lambda h: -kept[h]), {}
            for h in sorted(second, key=lambda h: -kept[h]):
                host = next((f for f in free if kept[f] + kept[h] <= n), None)
                if host is None:
                    break
                free.remove(host)
                mate[host] = h
            else:
                if best is None or len(firsts) < len(best[0]):
                    best = firsts, mate, t, extra
    firsts, mate, t, extra = best
    pairs = -(-len(firsts) // 2)
    per_owner = -(-pairs // n_plane) * 2
    n_small = per_owner // 2 * n_plane - pairs
    period = n_plane // n_small if n_small and n_plane % n_small == 0 else 0
    table = -np.ones((per_owner * n_plane, 3), np.int64)
    left = list(firsts)
    for owner in range(n_plane):
        count = per_owner - 2 if period and owner % period == period - 1 else per_owner
        for k in range(min(count, len(left))):
            h = left.pop(0)
            table[owner * per_owner + k] = h, mate.get(h, -1), kept[h]
    return table, per_owner, period, t, (extra or [-1])[0]


def tables(n, n_plane):
    width = n // n_plane
    cas = cas_table(n)
    rows, per_owner = packing(n, n_plane)[:2]
    order = sorted(range(n), key=lambda g: (min(g, n - g), g > n // 2))
    both = np.concatenate([cas[:, order], cas[:, order[::-1]]], 1)
    first, second = np.zeros((n, n), np.float32), np.zeros((n, n), np.float32)
    for row, (h, other, _) in enumerate(rows):
        if h >= 0:
            first[row] = cas[h]
        if other >= 0:
            second[row] = cas[other]
    wide = np.concatenate([both, pair_table(n, width), np.concatenate([first.T, second.T], 1) / n], 0)
    slim = np.concatenate([first, second, both.T / n, cas / n], 0)
    labels = np.full((n, 128), -7, np.int32)
    for row, (h, other, length) in enumerate(rows):
        place = row // per_owner * width + row % per_owner
        labels[place, 0] = h if h >= 0 else -7
        labels[place, 1] = other if other >= 0 else -7
    labels[:, 2] = n
    labels[: len(rows), 2] = np.where(rows[:, 2] < 0, n, rows[:, 2])
    return jnp.asarray(wide).astype(BF16), jnp.asarray(slim).astype(BF16), jnp.asarray(labels)


def dot(a, b):
    return jnp.dot(a, b, preferred_element_type=F32)


def broadcast_pieces(rows):
    return [(0, rows // 4), (rows // 4, rows // 4), (rows // 2, rows // 2)]


def far_first(count):
    return sorted(range(1, count), key=lambda d: -min(d, count - d))


def pick(index, values):
    out = values[0]
    for k in range(1, len(values)):
        out = jnp.where(index == k, values[k], out)
    return out


def remote(src, dst, send_sem, recv_sem, device):
    return pltpu.make_async_remote_copy(
        src_ref=src, dst_ref=dst, send_sem=send_sem, recv_sem=recv_sem,
        device_id=device, device_id_type=MESH,
    )


def kernel(
    n, n_plane,
    roots_ref, orb_hbm, wide_hbm, slim_hbm, labels_hbm, coulomb_hbm, ids_hbm, out_ref,
    orb, wide, slim, labels, coulomb, ids_ref,
    orb16, in_x0, in_x1, in_x2, sel0, sel1, sel2, in_y0, in_y1, in_y2,
    cand0, cand1, cand2, in_z0, in_z1, in_z2, shared,
    flat_sum, part, in_part, coul16, dense, grid_a, grid_b, send_f, recv_f, send_b, recv_b, total,
    s_orb, s_in, s_x, r_x, s_y, r_y, s_z, r_z, s_gy, r_gy, s_gx, r_gx,
    s_p, r_p, s_dy, r_dy, s_dx, r_dx, s_f, r_f, s_b, r_b,
):
    width = n // n_plane
    rows = width * n
    rows_g = rows // GROUPS
    _, per_owner, period, edge, edge_row = packing(n, n_plane)
    n_packed = per_owner * n_plane
    in_x, sel, in_y = [in_x0, in_x1, in_x2], [sel0, sel1, sel2], [in_y0, in_y1, in_y2]
    cand, in_z = [cand0, cand1, cand2], [in_z0, in_z1, in_z2]
    pieces = broadcast_pieces(rows)
    band, plane = lax.axis_index("band"), lax.axis_index("plane")
    y = lax.rem(band, NY)
    zh = lax.rem(band // NY, NZ)
    x = band // (NY * NZ)

    def at_band(bx, bz, by):
        return {"band": (bx * NZ + bz) * NY + by}

    def x_peer(d):
        return lax.rem(x + d, NX)

    def y_peer(d):
        return lax.rem(y + d, NY)

    def p_peer(d):
        return lax.rem(plane + d, n_plane)

    bits = [lax.rem(plane // (1 << k), 2) for k in range(n_plane.bit_length() - 1)]
    owners = []
    for flip in sorted(range(1, n_plane), key=lambda f: (-(f >> 1), f)):
        t = 0
        for k, bit in enumerate(bits):
            t = t + (1 << k) * (1 - bit if flip >> k & 1 else bit)
        owners.append(t)

    barrier = pltpu.get_barrier_semaphore()
    peers = [at_band(x_peer(d), zh, y) for d in far_first(NX)]
    peers += [at_band(x, zh, y_peer(d)) for d in far_first(NY)]
    peers += [at_band(x, lax.rem(zh + d, NZ), y) for d in range(1, NZ)]
    peers += [{"plane": p_peer(d)} for d in range(1, n_plane)]
    for peer in peers:
        pl.semaphore_signal(barrier, inc=1, device_id=peer, device_id_type=MESH)

    coul_rows = n // (NX * NY)
    first_row = (x * NY + y) * coul_rows
    coul_tile = pl.multiple_of(first_row // 16 * 16, 16)
    orb_loads = [
        pltpu.make_async_copy(orb_hbm.at[pl.ds(*at)], orb.at[pl.ds(*at)], s_orb.at[p])
        for p, at in enumerate(pieces)
    ]
    loads = [
        pltpu.make_async_copy(coulomb_hbm.at[pl.ds(coul_tile, 16)], coulomb, s_in.at[0]),
        pltpu.make_async_copy(ids_hbm, ids_ref, s_in.at[1]),
        pltpu.make_async_copy(labels_hbm, labels, s_in.at[2]),
        pltpu.make_async_copy(slim_hbm, slim, s_in.at[3]),
        pltpu.make_async_copy(wide_hbm, wide, s_in.at[4]),
    ]
    for load in orb_loads + loads:
        load.start()

    def round_piece(p):
        first, count = pieces[p]
        orb_loads[p].wait()
        orb16[first : first + count, :] = orb[first : first + count, :].astype(BF16)

    round_piece(0)
    pl.semaphore_wait(barrier, len(peers))

    def start(copy):
        copy.start()

    def arrived(region, sem):
        remote(region, region, sem, sem, {"plane": p_peer(1)}).wait_recv()

    def sent(region, sem):
        remote(region, region, sem, sem, {"plane": p_peer(1)}).wait_send()

    def x_copy(p, target, slot):
        first, count = pieces[p]
        chunk = count // NX
        return remote(
            orb16.at[pl.ds(first + target * chunk, chunk)], in_x[p].at[slot],
            s_x.at[p], r_x.at[p], at_band(target, zh, y),
        )

    def send_x(p):
        for d in far_first(NX):
            start(x_copy(p, x_peer(d), x))
        first, count = pieces[p]
        chunk = count // NX
        in_x[p][x] = orb16[pl.ds(first + x * chunk, chunk), :]

    root = [roots_ref[s] for s in range(STEPS)]
    root_y = [lax.rem(r, NY) for r in root]
    root_z = [lax.rem(r // NY, NZ) for r in root]
    root_x = [r // (NY * NZ) for r in root]

    def send_y(p):
        arrived(in_x[p].at[pl.ds(0, NX - 1)], r_x.at[p])
        for s in range(STEPS):
            sel[p][s] = pick(root_x[s], [in_x[p][k] for k in range(NX)])
        chunk = pieces[p][1] // (NX * NY)
        for d in far_first(NY):
            t = y_peer(d)
            start(remote(
                sel[p].at[:, pl.ds(t * chunk, chunk)], in_y[p].at[y],
                s_y.at[p], r_y.at[p], at_band(x, zh, t),
            ))
        in_y[p][y] = sel[p][:, pl.ds(y * chunk, chunk), :]

    def z_copy(p):
        return remote(
            cand[p], in_z[p], s_z.at[p], r_z.at[p], at_band(x, lax.rem(zh + 1, NZ), y)
        )

    def send_z(p):
        arrived(in_y[p].at[pl.ds(0, NY - 1)], r_y.at[p])
        for s in range(STEPS):
            cand[p][s] = pick(root_y[s], [in_y[p][k, s] for k in range(NY)])
        start(z_copy(p))

    def send_gy(p):
        z_copy(p).wait_recv()
        first, count = pieces[p]
        chunk = count // (NX * NY)
        at = pl.ds(first + (x * NY + y) * chunk, chunk)
        for s in range(STEPS):
            shared[s, at, :] = jnp.where(root_z[s] == zh, cand[p][s], in_z[p][s])
        block = shared.at[:, at]
        for d in far_first(NY):
            start(remote(block, block, s_gy.at[p], r_gy.at[p], at_band(x, zh, y_peer(d))))

    def wait_gy(p):
        first, count = pieces[p]
        chunk = count // (NX * NY)
        arrived(shared.at[:, pl.ds(first + x * NY * chunk, (NY - 1) * chunk)], r_gy.at[p])

    def send_gx(p, s):
        first, count = pieces[p]
        block = shared.at[s, pl.ds(first + x * (count // NX), count // NX)]
        for d in far_first(NX):
            start(remote(block, block, s_gx.at[p, s], r_gx.at[p, s], at_band(x_peer(d), zh, y)))

    def wait_gx(p, s):
        first, count = pieces[p]
        arrived(shared.at[s, pl.ds(first, count // NX * (NX - 1))], r_gx.at[p, s])

    def p_copy(target, slot):
        return remote(part.at[target], in_part.at[slot], s_p, r_p, {"plane": target})

    slots = ids_ref.shape[1]
    piece = -(-slots // (128 * PIECES)) * 128

    def add_part(i):
        if i == 0:
            loads[0].wait()
            loads[1].wait()
            loads[2].wait()
        at = slice(i * piece, min((i + 1) * piece, slots))
        ids = ids_ref[pl.ds(plane, 1), at]
        valid = ids >= 0
        id_h = jnp.where(valid, ids // n, -1)
        id_g = jnp.where(valid, lax.rem(ids, n), 0)
        lane = jnp.where(id_g == 0, 0, jnp.where(id_g <= n // 2, 2 * id_g - 1, 2 * (n - id_g)))
        reverse = (jnp.minimum(id_h, n - id_h) >= edge) | (id_h == edge_row)
        lane = jnp.where(reverse, n - 1 - lane, lane)
        iota = lax.broadcasted_iota(jnp.int32, (n, ids.shape[1]), 0)
        hot_h = (labels[:, 0:1] == id_h) | (labels[:, 1:2] == id_h)
        hot_g = jnp.where(iota == lane, 1.0, 0.0).astype(BF16)
        tile = coulomb[:, at].astype(F32)
        own = tile[:coul_rows]
        for k in range(1, 16 // coul_rows):
            inside = first_row - coul_tile == k * coul_rows
            own = jnp.where(inside, tile[k * coul_rows : (k + 1) * coul_rows], own)
        left = jnp.concatenate(
            [jnp.where(hot_h, own[k : k + 1], 0.0).astype(BF16) for k in range(coul_rows)], 0
        )
        flat = lax.dot_general(
            left, hot_g, (((1,), (1,)), ((), ())), preferred_element_type=F32
        )
        flat_sum[...] = flat if i == 0 else flat_sum[...] + flat

    def send_part():
        for k in range(coul_rows):
            for o in range(n_plane):
                at = slice(k * n + o * width, k * n + (o + 1) * width)
                part[o, k * width : (k + 1) * width, :] = flat_sum[at, :].astype(BF16)
        for t in owners:
            start(p_copy(t, plane))
        in_part[plane] = part[plane]

    coul_x, coul_y = rows // NX, rows // (NX * NY)

    def dy_copy(target, owner):
        block = coul16.at[pl.ds(x * coul_x + owner * coul_y, coul_y)]
        return remote(block, block, s_dy, r_dy, at_band(x, zh, target))

    def send_dy():
        arrived(in_part.at[pl.ds(0, n_plane - 1)], r_p)
        summed = in_part[0].astype(F32)
        for o in range(1, n_plane):
            summed = summed + in_part[o].astype(F32)
        coul16[pl.ds(x * coul_x + y * coul_y, coul_y), :] = summed.astype(BF16)
        for d in far_first(NY):
            start(dy_copy(y_peer(d), y))

    def dx_copy(target, owner):
        block = coul16.at[pl.ds(owner * coul_x, coul_x)]
        return remote(block, block, s_dx, r_dx, at_band(target, zh, y))

    def send_dx():
        arrived(coul16.at[pl.ds(x * coul_x, (NY - 1) * coul_y)], r_dy)
        for d in far_first(NX):
            start(dx_copy(x_peer(d), x))

    def wait_dense():
        arrived(coul16.at[pl.ds(0, (NX - 1) * coul_x)], r_dx)
        dense[...] = coul16[...].astype(F32)

    half = width // GROUPS
    block = per_owner * half
    small_block = block - 2 * half
    own_small = lax.rem(plane, period) == period - 1 if period else False
    n_small = n_plane // period if period else 0

    def sized(small, body):
        if not period:
            body(block)
            return
        pl.when(small)(lambda: body(small_block))
        pl.when(jnp.logical_not(small))(lambda: body(block))

    def of_owners(wait):
        every = block * (n_plane - 1) - 2 * half * n_small
        if not period:
            wait(orb16.at[pl.ds(0, every)])
            return
        pl.when(own_small)(lambda: wait(orb16.at[pl.ds(0, every + 2 * half)]))
        pl.when(jnp.logical_not(own_small))(lambda: wait(orb16.at[pl.ds(0, every)]))

    def of_own(wait):
        sized(own_small, lambda count: wait(orb16.at[pl.ds(0, count * (n_plane - 1))]))

    def send_block(from_ref, to_ref, count, sems, target):
        at = pl.ds(0, count)
        start(remote(from_ref.at[at], to_ref.at[at], sems[0], sems[1], {"plane": target}))

    def wait_group(g, s, i):
        if g == 0:
            wait_gx(i, s)
        elif i == 0:
            wait_gx(2, s)

    def forward(g, s):
        both = wide[:n, :]
        first, second = slim[:n_packed, :], slim[n : n + n_packed, :]
        in_first = lax.broadcasted_iota(jnp.int32, (n_packed, n), 1) < labels[:n_packed, 2:3]
        group = 4

        for i in range(half // group):
            wait_group(g, s, i)
            at = slice(g * rows_g + i * group * n, g * rows_g + (i + 1) * group * n)
            pair = (orb[at, :] * shared[s, at, :].astype(F32)).astype(BF16)
            along = dot(pair, both).astype(BF16)
            planes = [along[k * n : (k + 1) * n] for k in range(group)]
            from_first = dot(first, jnp.concatenate([plane_k[:, :n] for plane_k in planes], 1))
            from_second = dot(second, jnp.concatenate([plane_k[:, n:] for plane_k in planes], 1))
            for k in range(group):
                at = slice(k * n, (k + 1) * n)
                packed = jnp.where(in_first, from_first[:, at], from_second[:, at])
                grid_a[pl.ds(i * group + k, n_packed, stride=half), :] = packed
        for t in owners:
            send_f[s, g, t] = grid_a[pl.ds(pl.multiple_of(t * block, block), block), :].astype(BF16)
            small = lax.rem(t, period) == period - 1 if period else False
            sems = (s_f.at[g, s], r_f.at[g, s])
            sized(small, lambda count: send_block(
                send_f.at[s, g, t], recv_f.at[s, g, plane], count, sems, t))
        at = pl.ds(pl.multiple_of(plane * block, block), block)
        recv_f[s, g, plane] = grid_a[at, :].astype(BF16)

    def middle(s):
        for g in range(GROUPS):
            of_own(lambda region: arrived(region, r_f.at[g, s]))
        twin, cas = wide[n : 3 * n, :], slim[4 * n : 5 * n, :]
        pairs = per_owner // 2
        for first_pair in range(0, pairs, 2):
            js = range(first_pair, min(first_pair + 2, pairs))
            at = [slice(j * 2 * half, (j + 1) * 2 * half) for j in js]
            sticks = [recv_f[s, :, :, a, :].reshape(2 * n, n) for a in at]
            if period and js[-1] == pairs - 1:
                sticks[-1] = jnp.where(own_small, jnp.zeros_like(sticks[-1]), sticks[-1])
            spectrum = dot(twin, jnp.concatenate(sticks, 1))
            scaled = []
            for k, j in enumerate(js):
                for h in range(2):
                    coul = dense[pl.ds(2 * j + h, n, stride=width), :]
                    part_h = spectrum[h * n : (h + 1) * n, k * n : (k + 1) * n]
                    scaled.append((part_h * coul).astype(BF16))
            back = dot(cas, jnp.concatenate(scaled, 1))
            for k in range(len(js)):
                two = [
                    back[:, (2 * k + h) * n : (2 * k + h + 1) * n].reshape(n_plane, GROUPS, half, n)
                    for h in range(2)
                ]
                for g in range(GROUPS):
                    for q in range(n_plane):
                        both = jnp.concatenate([two[0][q, g], two[1][q, g]], 0)
                        send_b[s, g, q, at[k], :] = both.astype(BF16)
        for g in range(GROUPS):
            def send_all(count):
                for t in owners:
                    sems = (s_b.at[g, s], r_b.at[g, s])
                    send_block(send_b.at[s, g, t], recv_b.at[s, g, plane], count, sems, t)

            sized(own_small, send_all)
            recv_b[s, g, plane] = send_b[s, g, plane]

    def inverse(g, s):
        of_owners(lambda region: arrived(region, r_b.at[g, s]))
        first, second = wide[3 * n :, :n], wide[3 * n :, n:]
        both = slim[2 * n : 4 * n, :]
        in_first = lax.broadcasted_iota(jnp.int32, (n, n), 1) < labels[:, 2:3]
        grid_b[: n_packed * half, :] = recv_b[s, g].reshape(n_packed * half, n).astype(F32)
        group = 4

        for i in range(half // group):
            packed = [grid_b[pl.ds(i * group + k, n, stride=half), :] for k in range(group)]
            own = [jnp.where(in_first, one, 0.0).astype(BF16) for one in packed]
            other = [jnp.where(in_first, 0.0, one).astype(BF16) for one in packed]
            from_first = dot(first, jnp.concatenate(own, 1))
            from_second = dot(second, jnp.concatenate(other, 1))
            inverse_y = []
            for k in range(group):
                at = slice(k * n, (k + 1) * n)
                inverse_y.append(jnp.concatenate([from_first[:, at], from_second[:, at]], 1).astype(BF16))
            at = slice(g * rows_g + i * group * n, g * rows_g + (i + 1) * group * n)
            term = dot(jnp.concatenate(inverse_y, 0), both) * shared[s, at, :].astype(F32)
            if s == 0:
                total[at, :] = term
            else:
                out_ref[at, :] = (total[at, :] + term).astype(BF16)

    send_x(0)
    round_piece(1)
    send_x(1)
    round_piece(2)
    send_x(2)
    add_part(0)
    add_part(1)
    send_y(0)
    send_y(1)
    for i in range(2, PIECES):
        add_part(i)
    send_z(0)
    send_y(2)
    send_z(1)
    send_part()
    send_gy(0)
    send_z(2)
    send_gy(1)
    loads[3].wait()
    loads[4].wait()
    wait_gy(0)
    send_gx(0, 0)
    wait_gy(1)
    send_gx(1, 0)
    send_gy(2)
    send_gx(0, 1)
    send_gx(1, 1)
    send_dy()
    forward(0, 0)
    wait_gy(2)
    send_gx(2, 0)
    send_gx(2, 1)
    forward(0, 1)
    send_dx()
    forward(1, 0)
    forward(1, 1)
    for p, (_, count) in enumerate(pieces):
        sent(in_x[p].at[pl.ds(0, NX - 1)], s_x.at[p])
        sent(in_y[p].at[pl.ds(0, NY - 1)], s_y.at[p])
        sent(in_z[p], s_z.at[p])
        sent(shared.at[:, pl.ds(0, (NY - 1) * (count // (NX * NY)))], s_gy.at[p])
        for s in range(STEPS):
            sent(shared.at[s, pl.ds(0, (NX - 1) * (count // NX))], s_gx.at[p, s])
    sent(in_part.at[pl.ds(0, n_plane - 1)], s_p)
    grid_b[n_packed * half :, :] = jnp.zeros(((n - n_packed) * half, n), F32)
    for q in range(n_plane):
        if period and q % period == period - 1:
            recv_b[:, :, q, small_block:, :] = jnp.zeros((STEPS, GROUPS, 2 * half, n), BF16)
    wait_dense()
    middle(0)
    sent(coul16.at[pl.ds(0, (NY - 1) * coul_y)], s_dy)
    sent(coul16.at[pl.ds(0, (NX - 1) * coul_x)], s_dx)
    middle(1)
    for g in range(GROUPS):
        for s in range(STEPS):
            of_owners(lambda region: sent(region, s_f.at[g, s]))
    inverse(0, 0)
    inverse(1, 0)
    inverse(0, 1)
    inverse(1, 1)
    for g in range(GROUPS):
        for s in range(STEPS):
            of_own(lambda region: sent(region, s_b.at[g, s]))


def on_device(orbitals, coulomb, stick_lists, roots):
    _, width, n, _ = orbitals.shape
    n_plane = n // width
    rows = width * n
    rows_g = rows // GROUPS
    counts = [count for _, count in broadcast_pieces(rows)]
    coul_block = n // (NX * NY) * width
    per_owner = packing(n, n_plane)[1]
    wide, slim, labels = tables(n, n_plane)
    hbm = pl.BlockSpec(memory_space=pl.ANY)
    vmem = pl.BlockSpec(memory_space=pltpu.VMEM)
    dma = pltpu.SemaphoreType.DMA

    def pair_of_sems(*shape):
        return [dma(shape), dma(shape)]

    gs = (GROUPS, STEPS)
    spectra = pltpu.VMEM((STEPS, GROUPS, n_plane, per_owner * width // GROUPS, n), BF16)
    out = pl.pallas_call(
        functools.partial(kernel, n, n_plane),
        out_shape=jax.ShapeDtypeStruct((rows, n), BF16),
        in_specs=[pl.BlockSpec(memory_space=pltpu.SMEM)] + [hbm] * 6,
        out_specs=vmem,
        scratch_shapes=[
            pltpu.VMEM((rows, n), F32),
            pltpu.VMEM(wide.shape, BF16),
            pltpu.VMEM(slim.shape, BF16),
            pltpu.VMEM(labels.shape, jnp.int32),
            pltpu.VMEM((16, coulomb.shape[1]), BF16),
            pltpu.VMEM(stick_lists.shape, jnp.int32),
            pltpu.VMEM((rows, n), BF16),
            *[pltpu.VMEM((NX, count // NX, n), BF16) for count in counts],
            *[pltpu.VMEM((STEPS, count // NX, n), BF16) for count in counts],
            *[pltpu.VMEM((NY, STEPS, count // (NX * NY), n), BF16) for count in counts],
            *[pltpu.VMEM((STEPS, count // (NX * NY), n), BF16) for count in counts * 2],
            pltpu.VMEM((STEPS, rows, n), BF16),
            pltpu.VMEM((n // (NX * NY) * n, n), F32),
            pltpu.VMEM((n_plane, coul_block, n), BF16),
            pltpu.VMEM((n_plane, coul_block, n), BF16),
            pltpu.VMEM((rows, n), BF16),
            pltpu.VMEM((rows, n), F32),
            pltpu.VMEM((rows_g, n), F32),
            pltpu.VMEM((rows_g, n), F32),
            spectra, spectra, spectra, spectra,
            pltpu.VMEM((rows, n), F32),
            dma((len(counts),)),
            dma((5,)),
            *pair_of_sems(len(counts)),
            *pair_of_sems(len(counts)),
            *pair_of_sems(len(counts)),
            *pair_of_sems(len(counts)),
            *pair_of_sems(len(counts), STEPS),
            dma, dma, dma, dma, dma, dma,
            *pair_of_sems(*gs),
            *pair_of_sems(*gs),
        ],
        compiler_params=pltpu.CompilerParams(
            collective_id=0, has_side_effects=True, vmem_limit_bytes=57 * 1024 * 1024
        ),
        name="exchange",
    )(
        roots, orbitals.reshape(rows, n),
        wide, slim, labels, coulomb, stick_lists,
    )
    return out.reshape(1, width, n, n)


def solution(mesh):
    in_specs = (P("band", "plane", None, None), P(None, "plane"), P(), P())
    out_specs = P("band", "plane", None, None)
    return jax.shard_map(
        on_device, mesh=mesh, in_specs=in_specs, out_specs=out_specs, check_vma=False
    )
```

profile of v0, /device:TPU:1, one launch (start us, length us, event | category | flops | bytes accessed | tf_op | source)
XLA Modules:
  0.0 81.1 jit_solution(13465937709639195131)
XLA Ops:
  0.0 79.2 %exchange.1 = bf16[2048,128]{1,0:T(8,128)(2,1)} custom-call(s32[2]{0:T(128)} %roots_ref.1, f32[2048,128]{1,0:T(8,128)} %bitcast.3, bf16[512,256]{1,0:T(8,128)(2,1)} %constant.10.wide_hbm, bf16[640,128]{1,0:T(8,128)(2,1)} %constant.11.slim_hbm, s32[128,128]{1,0:T(8,128)} %constant.8.clone.labels_hbm, bf16[128,2688]{1,0:T(8,128)(2,1)} %coulomb_hbm.1, ...), custom_call_target="tpu_custom_call" | custom-call | tf_op jit(solution)/shard_map/exchange/pallas_call | solution.py:554
  79.3 1.9 %copy.9 = bf16[1,16,128,128]{3,2,1,0:T(8,128)(2,1)} copy(bf16[1,16,128,128]{3,2,1,0:T(8,128)(2,1)} %bitcast.2) | data formatting | bytes 1048576
where the time goes:
time: 81.3 us; the launch traced here: 81.1 us
  Pallas kernels  79.2 us (97%)
  local copies, waits for them, and re-layouts  1.89 us (2%)
    pallas_call x1, Pallas kernels, on_device(): pl.pallas_call(functools.partial(kernel, n, n_plane), out_shape=jax.Shape...  79.2 us
    unnamed x1, local copies, waits for them, and re-layouts  1.89 us

commit v1 on v0

--- a/solution.py
+++ b/solution.py
@@ -97,7 +97,7 @@
 
 
 def broadcast_pieces(rows):
-    return [(0, rows // 4), (rows // 4, rows // 4), (rows // 2, rows // 2)]
+    return [(0, rows // 2), (rows // 2, rows // 2)]
 
 
 def far_first(count):
@@ -122,8 +122,7 @@
     n, n_plane,
     roots_ref, orb_hbm, wide_hbm, slim_hbm, labels_hbm, coulomb_hbm, ids_hbm, out_ref,
     orb, wide, slim, labels, coulomb, ids_ref,
-    orb16, in_x0, in_x1, in_x2, sel0, sel1, sel2, in_y0, in_y1, in_y2,
-    cand0, cand1, cand2, in_z0, in_z1, in_z2, shared,
+    orb16, in_x0, in_x1, sel0, sel1, in_y0, in_y1, cand0, cand1, in_z0, in_z1, shared,
     flat_sum, part, in_part, coul16, dense, grid_a, grid_b, send_f, recv_f, send_b, recv_b, total,
     s_orb, s_in, s_x, r_x, s_y, r_y, s_z, r_z, s_gy, r_gy, s_gx, r_gx,
     s_p, r_p, s_dy, r_dy, s_dx, r_dx, s_f, r_f, s_b, r_b,
@@ -133,8 +132,8 @@
     rows_g = rows // GROUPS
     _, per_owner, period, edge, edge_row = packing(n, n_plane)
     n_packed = per_owner * n_plane
-    in_x, sel, in_y = [in_x0, in_x1, in_x2], [sel0, sel1, sel2], [in_y0, in_y1, in_y2]
-    cand, in_z = [cand0, cand1, cand2], [in_z0, in_z1, in_z2]
+    in_x, sel, in_y = [in_x0, in_x1], [sel0, sel1], [in_y0, in_y1]
+    cand, in_z = [cand0, cand1], [in_z0, in_z1]
     pieces = broadcast_pieces(rows)
     band, plane = lax.axis_index("band"), lax.axis_index("plane")
     y = lax.rem(band, NY)
@@ -374,10 +373,8 @@
         start(remote(from_ref.at[at], to_ref.at[at], sems[0], sems[1], {"plane": target}))
 
     def wait_group(g, s, i):
-        if g == 0:
-            wait_gx(i, s)
-        elif i == 0:
-            wait_gx(2, s)
+        if i == 0:
+            wait_gx(g, s)
 
     def forward(g, s):
         both = wide[:n, :]
@@ -471,20 +468,14 @@
     send_x(0)
     round_piece(1)
     send_x(1)
-    round_piece(2)
-    send_x(2)
-    add_part(0)
-    add_part(1)
+    for i in range(PIECES):
+        add_part(i)
     send_y(0)
+    send_part()
     send_y(1)
-    for i in range(2, PIECES):
-        add_part(i)
     send_z(0)
-    send_y(2)
     send_z(1)
-    send_part()
     send_gy(0)
-    send_z(2)
     send_gy(1)
     loads[3].wait()
     loads[4].wait()
@@ -492,17 +483,13 @@
     send_gx(0, 0)
     wait_gy(1)
     send_gx(1, 0)
-    send_gy(2)
+    send_dy()
+    forward(0, 0)
     send_gx(0, 1)
     send_gx(1, 1)
-    send_dy()
-    forward(0, 0)
-    wait_gy(2)
-    send_gx(2, 0)
-    send_gx(2, 1)
+    forward(1, 0)
+    send_dx()
     forward(0, 1)
-    send_dx()
-    forward(1, 0)
     forward(1, 1)
     for p, (_, count) in enumerate(pieces):
         sent(in_x[p].at[pl.ds(0, NX - 1)], s_x.at[p])
@@ -590,7 +577,7 @@
             *pair_of_sems(*gs),
         ],
         compiler_params=pltpu.CompilerParams(
-            collective_id=0, has_side_effects=True, vmem_limit_bytes=57 * 1024 * 1024
+            collective_id=0, has_side_effects=True, vmem_limit_bytes=53760 * 1024
         ),
         name="exchange",
     )(

time: 81.3 us -> 85.8 us (1.055)
  local copies, waits for them, and re-layouts: 1.89 us -> 5.04 us
  Pallas kernels: 79.2 us -> 80.5 us
    unnamed x1 -> x11, local copies, waits for them, and re-layouts: 1.89 us -> 5.04 us
    pallas_call x1, Pallas kernels: 79.2 us -> 80.5 us  [on_device(): pl.pallas_call(functools.partial(kernel, n, n_plane), out_shape=jax.Shape...]
where the time goes in v1:
time: 85.8 us; the launch traced here: 85.5 us
  Pallas kernels  80.5 us (94%)
  local copies, waits for them, and re-layouts  5.04 us (6%)
    pallas_call x1, Pallas kernels, on_device(): pl.pallas_call(functools.partial(kernel, n, n_plane), out_shape=jax.Shape...  80.5 us
    unnamed x11, local copies, waits for them, and re-layouts  5.04 us

profile of v1, /device:TPU:1, one launch (start us, length us, event | category | flops | bytes accessed | tf_op | source)
XLA Modules:
  0.0 85.5 jit_solution(1169723098422059708)
XLA Ops:
  0.0 0.0 copy-start.4
  0.0 0.7 copy-done.4
  0.7 0.0 copy-start
  0.7 0.9 %copy-done = bf16[512,256]{1,0:T(8,128)(2,1)S(1)} copy-done((bf16[512,256]{1,0:T(8,128)(2,1)S(1)}, bf16[512,256]{1,0:T(8,128)(2,1)}, u32[]{:S(2)}) %copy-start) | copy-done | bytes 262168
  1.6 0.0 copy-start.1
  1.6 0.9 %copy-done.1 = bf16[640,128]{1,0:T(8,128)(2,1)S(1)} copy-done((bf16[640,128]{1,0:T(8,128)(2,1)S(1)}, bf16[640,128]{1,0:T(8,128)(2,1)}, u32[]{:S(2)}) %copy-start.1) | copy-done | bytes 163864
  2.5 0.0 copy-start.2
  2.5 0.9 %copy-done.2 = s32[8,2688]{1,0:T(8,128)S(1)} copy-done((s32[8,2688]{1,0:T(8,128)S(1)}, s32[8,2688]{1,0:T(8,128)}, u32[]{:S(2)}) %copy-start.2) | copy-done | bytes 86040
  3.4 0.0 copy-start.3
  3.4 0.8 copy-done.3
  4.3 80.5 %exchange.1 = bf16[2048,128]{1,0:T(8,128)(2,1)S(1)} custom-call(s32[2]{0:T(128)S(1)} %copy-done.4, f32[2048,128]{1,0:T(8,128)} %bitcast.3, bf16[512,256]{1,0:T(8,128)(2,1)S(1)} %copy-done, bf16[640,128]{1,0:T(8,128)(2,1)S(1)} %copy-done.1, s32[128,128]{1,0:T(8,128)S(1)} %copy-done.3, bf16[128,2688]{1,0:T(8,128)(2,1)} %coulomb_hbm.1, s32[8,2688]{1,0:T(8,128)S(1)} %copy-done.2), custom_call_target="tpu_custom_call" | custom-call | tf_op jit(solution)/shard_map/exchange/pallas_call | solution.py:541
  84.7 0.8 copy.9
Async XLA Ops:
  0.0 0.7 copy-start.4
  0.7 0.9 %copy-start = (bf16[512,256]{1,0:T(8,128)(2,1)S(1)}, bf16[512,256]{1,0:T(8,128)(2,1)}, u32[]{:S(2)}) copy-start(bf16[512,256]{1,0:T(8,128)(2,1)} %constant.10.wide_hbm) | copy-start | bytes 786436
  1.6 0.9 %copy-start.1 = (bf16[640,128]{1,0:T(8,128)(2,1)S(1)}, bf16[640,128]{1,0:T(8,128)(2,1)}, u32[]{:S(2)}) copy-start(bf16[640,128]{1,0:T(8,128)(2,1)} %constant.11.slim_hbm) | copy-start | bytes 491524
  2.5 0.9 %copy-start.2 = (s32[8,2688]{1,0:T(8,128)S(1)}, s32[8,2688]{1,0:T(8,128)}, u32[]{:S(2)}) copy-start(s32[8,2688]{1,0:T(8,128)} %ids_hbm.1) | copy-start | bytes 258052
  3.4 0.8 copy-start.3
